TPU v7x, 256 devices: a whole 4x4x8 slice. The times are simulated.
256 devices in a mesh: dp: 64 (over x, z, core), mp: 4 (over y).
Axes of the slice: x: 4, y: 4, z: 8, core: 2. Of those that a mesh axis runs over, the one named last changes fastest.
Arguments:
- activations: bfloat16 [32768, 2560], P('dp'), may hold values from -6 to 6
- cotangent: bfloat16 [32768, 6912], P('dp', 'mp'), may hold values from -6 to 6
- frozen_weight: bfloat16 [2560, 6912], P(None, 'mp'), may hold values from -0.078125 to 0.078125
- skew_params: bfloat16 [10, 256, 256], replicated, may hold values from -0.125 to 0.125
- tile_order: int32 [20], replicated, may hold values from 0 to 19, each once
- block_owner: int32 [10], replicated, may hold values from 0 to 63, as said below
Outputs:
- input_grad: bfloat16 [32768, 2560], P('dp', 'mp')
- skew_grads: float32 [192, 256, 256], P('dp')
Inputs may be any that keep to these rules, and one draw needn't show every extreme that they name: `tile_order`: a permutation of the 20 tiles. `block_owner`: no index of dp owns more than 3 blocks, and some index owns exactly 3; indices 0 and 64 - 1 own blocks in every draw.
All inputs are finite; a program needn't handle non-finite values.
Results may differ from a plain program's by a relative error of at most 0.001.
Values sent between devices are 32-bit elements; how exact they have to be, the bound alone decides.
No kernel may reach another device: no remote copies, remote signals or barrier semaphores. Data moves between devices by JAX's collectives and lax.ppermute only.
A program may use at most 128 MiB of HBM per device.

v0:
```python
import math
import jax
import jax.numpy as jnp
from jax import lax
from jax.sharding import PartitionSpec as P

SLOTS = 3
highest = lax.Precision.HIGHEST


def product(first, second):
    return jnp.einsum("bij,bjk->bik", first, second, precision=highest)


def cayley_parts(params):
    plain = params.astype(jnp.float32)
    skew = plain - jnp.swapaxes(plain, 1, 2)
    square = product(skew, skew)
    cube = product(square, skew)
    identity = jnp.eye(skew.shape[1], dtype=jnp.float32)
    return (skew, identity[None] + 2.0 * skew + 2.0 * square + cube)


def to_blocks(matrix, order, tile_count, block_count):
    tiled = matrix.reshape(matrix.shape[0], tile_count, -1)
    return jnp.take(tiled, order, axis=1).reshape(matrix.shape[0], block_count, -1)


def inverse_order(order, tile_count):
    positions = jnp.arange(tile_count, dtype=jnp.int32)
    matches = (order[:, None] == positions[None, :]).astype(jnp.int32)
    return jnp.sum(positions[:, None] * matches, axis=0)


def adjoint(gram, skew):
    transposed = jnp.swapaxes(skew, 1, 2)
    left = product(gram, transposed)
    right = product(transposed, gram)
    total = (
        2.0 * gram
        + 2.0 * (left + right)
        + product(left, transposed)
        + product(transposed, left)
        + product(transposed, right)
    )
    return total - jnp.swapaxes(total, 1, 2)


def local(activations, cotangent, frozen_weight, skew_params, tile_order, block_owner):
    token_rows = activations.shape[0]
    tile_count = tile_order.shape[0]
    block_count = block_owner.shape[0]
    skew, rotation = cayley_parts(skew_params)
    partial_grad = lax.dot_general(
        cotangent, frozen_weight, (((1,), (1,)), ((), ())), preferred_element_type=jnp.float32
    )
    feature_grad = lax.psum(partial_grad, "mp")
    grad_blocks = to_blocks(feature_grad, tile_order, tile_count, block_count)
    own_tiles = tile_count // lax.axis_size("mp")
    inverse = inverse_order(tile_order, tile_count)
    own_places = lax.dynamic_slice_in_dim(inverse, lax.axis_index("mp") * own_tiles, own_tiles, 0)
    half_rows = rotation.reshape(block_count * 2, rotation.shape[1] // 2, rotation.shape[2])
    own_rotation = jnp.take(half_rows, own_places, axis=0)
    own_blocks = jnp.take(grad_blocks, own_places // 2, axis=1)
    own_rotated = jnp.einsum("tkj,kij->tki", own_blocks, own_rotation, precision=highest)
    input_grad = own_rotated.reshape(token_rows, -1).astype(jnp.bfloat16)
    quarter = token_rows // lax.axis_size("mp")
    row_start = lax.axis_index("mp") * quarter
    some_inputs = lax.dynamic_slice_in_dim(activations, row_start, quarter, 0)
    input_blocks = to_blocks(some_inputs, tile_order, tile_count, block_count).astype(jnp.float32)
    some_grads = lax.dynamic_slice_in_dim(grad_blocks, row_start, quarter, 0)
    local_gram = jnp.einsum("tbi,tbj->bij", input_blocks, some_grads, precision=highest)
    gram = lax.psum(local_gram, ("dp", "mp"))
    owned = (block_owner == lax.axis_index("dp")).astype(jnp.int32)
    ranking = jnp.cumsum(owned) - 1
    slot_ids = jnp.arange(SLOTS, dtype=jnp.int32)
    selector = ((owned[None, :] == 1) & (ranking[None, :] == slot_ids[:, None])).astype(jnp.float32)
    gram_slots = jnp.einsum("sb,bij->sij", selector, gram, precision=highest)
    skew_slots = jnp.einsum("sb,bij->sij", selector, skew, precision=highest)
    scaling = 1.0 / math.sqrt(token_rows * lax.axis_size("dp"))
    skew_grads = adjoint(gram_slots, skew_slots) * scaling
    return (input_grad, skew_grads)


def solution(mesh):
    placed = (P("dp", None), P("dp", "mp"), P(None, "mp"), P(), P(), P())
    return jax.shard_map(
        local,
        mesh=mesh,
        in_specs=placed,
        out_specs=(P("dp", "mp"), P("dp", None, None)),
        check_vma=False,
    )
```

profile of v0, /device:TPU:2, one launch (start us, length us, event | category | flops | bytes accessed | tf_op | source)
XLA Modules:
  0.0 453.6 jit_solution(274264501818761207)
XLA Ops:
  7.2 0.0 copy-start
  7.2 0.0 all-reduce.3.cloned.1.call-start
  7.2 11.4 %fusion.34 = f32[512,2560]{0,1:T(8,128)} fusion(bf16[512,1728]{0,1:T(8,128)(2,1)} %param.7, bf16[2560,1728]{0,1:T(8,128)(2,1)} %param.8), kind=kOutput, calls=%fused_computation.62 | convolution fusion | flops 4529848320 | bytes 15859712 | tf_op jit(solution)/shard_map/dot_general | solution.py:54
  18.7 5.9 %copy.80 = f32[512,20,128]{2,0,1:T(8,128)} copy(f32[512,20,128]{0,2,1:T(8,128)} %bitcast.49) | data formatting | bytes 10485760 | tf_op jit(solution)/shard_map/reshape | solution.py:25
  24.6 0.0 all-reduce.3.cloned.1.call-update
  24.6 0.0 all-reduce.5.cloned.1.call-start
  24.7 0.6 copy-done.5
  25.3 0.2 reduce-window.8
  25.5 0.1 broadcast_in_dim.63
  25.5 0.1 broadcast_in_dim.64
  25.7 0.1 constant_dynamic-slice_fusion
  25.7 0.3 copy.100
  26.1 0.3 copy.84
  26.4 0.7 gather_fusion.3
  27.1 0.3 copy.85
  27.4 1.6 copy.77
  29.1 1.9 copy.78
  31.0 0.1 select_reduce_fusion
  31.1 0.1 compare_and_fusion.2
  31.2 0.5 bitcast_select_fusion
  31.7 2.4 bitcast_subtract_fusion
  34.1 3.9 fusion
  38.0 104.7 %all-reduce.3.cloned.1.call-done = f32[512,20,128]{2,0,1:T(8,128)} async-done(((f32[512,20,128]{2,0,1:T(8,128)}), f32[512,20,128]{2,0,1:T(8,128)}) %all-reduce.3.cloned.1.call-update) | async-done | bytes 5242896 | tf_op jit(solution)/shard_map/psum | solution.py:57
  142.7 5.7 %gather_fusion.1 = f32[20,512,128]{2,1,0:T(8,128)} fusion(f32[512,20,128]{2,0,1:T(8,128)} %all-reduce.3.cloned.1.call-done, s32[1024]{0:T(1024)S(1)} %pad_clamp_fusion.1), kind=kCustom, calls=%fused_computation.1 | custom fusion | bytes 10485840 | tf_op jit(solution)/shard_map/jit(_take)/gather | solution.py:26
  148.4 5.9 %copy.81 = f32[512,20,128]{0,2,1:T(8,128)} copy(f32[512,20,128]{2,0,1:T(8,128)} %bitcast.47) | data formatting | bytes 10485760 | tf_op jit(solution)/shard_map/jit(_take)/gather | solution.py:26
  154.3 5.9 %copy.82 = f32[512,10,256]{2,0,1:T(8,128)} copy(f32[512,10,256]{0,2,1:T(8,128)} %bitcast.48) | data formatting | bytes 10485760 | tf_op jit(solution)/shard_map/jit(_take)/gather | solution.py:26
  160.2 2.9 broadcast_select_fusion
  163.1 2.3 copy-done.2
  165.4 2.8 fusion.11
  168.2 0.0 all-reduce.5.cloned.1.call-update
  168.3 1.5 copy.90
  169.8 2.9 fusion.33
  172.7 4.8 %add_add_fusion = f32[10,256,256]{2,1,0:T(8,128)} fusion(f32[10,256,256]{2,1,0:T(8,128)S(1)} %fusion.33, f32[10,256,256]{2,1,0:T(8,128)S(1)} %bitcast_subtract_fusion, f32[256,256]{1,0:T(8,128)S(1)} %fusion.24), kind=kOutput, calls=%fused_computation.13 | convolution fusion | flops 2016542720 | bytes 8126464 | tf_op jit(solution)/shard_map/bij,bjk->bik/dot_general | solution.py:12
  177.4 3.2 gather_fusion
  180.6 3.2 gather_fusion.2
  183.8 4.7 %fusion.7 = bf16[5,128,512]{2,1,0:T(8,128)(2,1)} fusion(f32[5,512,256]{2,1,0:T(8,128)S(1)} %gather_fusion.2, pred[5]{0:T(512)(128)(4,1)S(1)} %get-tuple-element.16, f32[5,128,256]{2,1,0:T(8,128)} %gather_fusion, pred[5]{0:T(512)(128)(4,1)S(1)} %get-tuple-element.10), kind=kOutput, calls=%fused_computation.14 | convolution fusion | flops 1007779840 | bytes 3932170 | tf_op jit(solution)/shard_map/tkj,kij->tki/dot_general | solution.py:65
  188.5 2.2 copy.97
  190.7 240.4 %all-reduce.5.cloned.1.call-done = f32[10,256,256]{2,1,0:T(8,128)} async-done(((f32[10,256,256]{2,1,0:T(8,128)}), f32[10,256,256]{2,1,0:T(8,128)}) %all-reduce.5.cloned.1.call-update) | async-done | bytes 2621456 | tf_op jit(solution)/shard_map/psum | solution.py:73
  431.1 4.8 %fusion.2 = f32[3,256,256]{2,0,1:T(4,128)S(1)} fusion(f32[10,256,256]{2,1,0:T(8,128)} %all-reduce.5.cloned.1.call-done, s32[10]{0:T(128)S(1)} %add_bitcast_fusion, pred[10]{0:T(512)(128)(4,1)S(1)} %get-tuple-element.14), kind=kOutput, calls=%fused_computation.6 | convolution fusion | flops 23593020 | bytes 3407922 | tf_op jit(solution)/shard_map/sb,bij->sij/dot_general | solution.py:78
  436.0 1.0 fusion.17
  437.0 1.0 fusion.19
  438.0 1.1 convolution_add_fusion.2
  439.1 0.9 convolution_add_fusion.1
  440.1 0.0 copy-start.1
  440.1 1.8 convolution_add_fusion
  441.9 2.3 copy.96
  444.2 1.5 fusion.14
  445.6 1.1 copy.98
  (19 shorter events, 0.1 us)
Async XLA Ops:
  7.2 18.5 %copy-start = (bf16[512,2560]{1,0:T(8,128)(2,1)S(1)}, bf16[512,2560]{1,0:T(8,128)(2,1)}, u32[]{:S(2)}) copy-start(bf16[512,2560]{1,0:T(8,128)(2,1)} %param.6) | copy-start | bytes 7864324
  7.2 135.6 %all-reduce.3.cloned.1.call-start = ((), (), s32[]{:S(2)}) async-start(), calls=%async_computation | async-start | bytes 10485760 | tf_op jit(solution)/shard_map/psum | solution.py:57
  24.6 0.7 copy-start.5
  24.6 0.8 copy-start.6
  24.6 406.5 %all-reduce.5.cloned.1.call-start = ((), (), s32[]{:S(2)}) async-start(), calls=%async_computation.1 | async-start | bytes 5242880 | tf_op jit(solution)/shard_map/psum | solution.py:73
  29.0 2.1 copy-start.4
  163.1 2.3 copy-start.2
  190.7 245.2 %copy-start.3 = (f32[3,256,256]{2,0,1:T(4,128)S(1)}, f32[3,256,256]{2,0,1:T(4,128)}, u32[]{:S(2)}) copy-start(f32[3,256,256]{2,0,1:T(4,128)} %fusion) | copy-start | bytes 2359300
  440.1 6.7 %copy-start.1 = (bf16[512,2560]{1,0:T(8,128)(2,1)S(1)}, bf16[512,2560]{1,0:T(8,128)(2,1)}, u32[]{:S(2)}) copy-start(bf16[512,2560]{1,0:T(8,128)(2,1)} %param.6) | copy-start | bytes 7864324
Sparse Core Ops, SparseCore 0:
  24.7 117.9 all-reduce.2
  168.4 262.7 all-reduce.4
where the time goes:
time: 454 us
  waiting for transfers between devices  345 us (76%)
  local copies, waits for them, and re-layouts  45.2 us (10%)
  matrix products  41.2 us (9%)
  between operations  14.3 us (3%)
  other arithmetic  7.66 us (2%)
    psum x1, waiting for transfers between devices, local(): gram = lax.psum(local_gram, ('dp', 'mp'))  240 us
    psum x1, waiting for transfers between devices, local(): feature_grad = lax.psum(partial_grad, 'mp')  105 us
    gather x5, local copies, waits for them, and re-layouts, to_blocks(): jnp.take(tiled, order, axis=1).reshape(matrix.shape[0], block_count, -1)  18.5 us
    dot_general x7, matrix products, product(): return jnp.einsum('bij,bjk->bik', first, second, precision=highest)  13.5 us
    dot_general x1, matrix products, local(): lax.dot_general(cotangent, frozen_weight, (((1,), (1,)), ((), ())), prefe...  11.4 us
  transfers between devices with their start and end apart: 2, of which 2 were waited for; matrix products, arithmetic and copies ran while one was open for 8% of the time, Pallas kernels for 0%

commit v1 on v0

--- a/solution.py
+++ b/solution.py
@@ -54,7 +54,11 @@
     partial_grad = lax.dot_general(
         cotangent, frozen_weight, (((1,), (1,)), ((), ())), preferred_element_type=jnp.float32
     )
-    feature_grad = lax.psum(partial_grad, "mp")
+    feature_grad = partial_grad
+    for hop in (1, 2):
+        feature_grad = feature_grad + lax.ppermute(
+            feature_grad, "mp", [(dev, dev ^ hop) for dev in range(4)]
+        )
     grad_blocks = to_blocks(feature_grad, tile_order, tile_count, block_count)
     own_tiles = tile_count // lax.axis_size("mp")
     inverse = inverse_order(tile_order, tile_count)

time: 454 us -> 583 us (1.28)
  waiting for transfers between devices: 345 us -> 456 us
  other arithmetic: 7.66 us -> 18.3 us
    ppermute x0 -> x2, waiting for transfers between devices: none -> 213 us  [local(): lax.ppermute(feature_grad, 'mp', [(dev, dev ^ hop) for dev in range(4)])]
    psum x1 -> x0, waiting for transfers between devices: 105 us -> none  [local(): feature_grad = lax.psum(partial_grad, 'mp')]
    add x0 -> x2, other arithmetic: none -> 10.6 us  [local(): feature_grad + lax.ppermute(feature_grad, 'mp', [(dev, dev ^ hop) for dev...]
    add x0 -> x1, local copies, waits for them, and re-layouts: none -> 5.9 us  [local(): feature_grad + lax.ppermute(feature_grad, 'mp', [(dev, dev ^ hop) for dev...]
  transfers between devices with their start and end apart: 2 -> 3, of which waited for: 2 -> 3; matrix products, arithmetic and copies ran while one was open for 8% -> 6% of each run, Pallas kernels for 0% -> 0%
where the time goes in v1:
time: 583 us
  waiting for transfers between devices  456 us (78%)
  local copies, waits for them, and re-layouts  50.7 us (9%)
  matrix products  38 us (7%)
  other arithmetic  18.3 us (3%)
  between operations  14.3 us (2%)
    psum x1, waiting for transfers between devices, local(): gram = lax.psum(local_gram, ('dp', 'mp'))  243 us
    ppermute x2, waiting for transfers between devices, local(): lax.ppermute(feature_grad, 'mp', [(dev, dev ^ hop) for dev in range(4)])  213 us
    gather x5, local copies, waits for them, and re-layouts, to_blocks(): jnp.take(tiled, order, axis=1).reshape(matrix.shape[0], block_count, -1)  18.5 us
    dot_general x7, matrix products, product(): return jnp.einsum('bij,bjk->bik', first, second, precision=highest)  13.5 us
  transfers between devices with their start and end apart: 3, of which 3 were waited for; matrix products, arithmetic and copies ran while one was open for 6% of the time, Pallas kernels for 0%

profile of v1, /device:TPU:2, one launch (start us, length us, event | category | flops | bytes accessed | tf_op | source)
XLA Modules:
  0.0 582.6 jit_solution(14605904334856753786)
XLA Ops:
  7.2 0.0 all-reduce.2.cloned.1.call-start
  7.2 8.3 %fusion.34 = f32[512,2560]{1,0:T(8,128)S(1)} fusion(bf16[512,1728]{0,1:T(8,128)(2,1)} %param.7, bf16[2560,1728]{0,1:T(8,128)(2,1)} %param.8), kind=kOutput, calls=%fused_computation.62 | convolution fusion | flops 4529848320 | bytes 15859712 | tf_op jit(solution)/shard_map/dot_general | solution.py:54
  15.5 1.7 collective-permute-start
  17.2 113.2 %collective-permute-done = f32[512,2560]{1,0:T(8,128)S(1)} collective-permute-done((f32[512,2560]{1,0:T(8,128)S(1)}, f32[512,2560]{1,0:T(8,128)S(1)}, u32[]{:S(2)}, u32[]{:S(2)}) %collective-permute-start) | collective-permute-done | bytes 5242912 | tf_op jit(solution)/shard_map/ppermute | solution.py:59
  130.4 3.3 add.88
  133.7 3.2 collective-permute-start.1
  136.9 0.3 copy.99
  137.2 0.3 copy.84
  137.6 0.7 gather_fusion.3
  138.3 0.3 copy.85
  138.7 0.1 broadcast_in_dim.63
  138.7 0.1 broadcast_in_dim.64
  138.9 0.2 reduce-window.8
  139.1 1.6 copy.77
  140.7 1.9 copy.78
  142.6 0.1 select_reduce_fusion
  142.7 0.1 compare_and_fusion.2
  142.8 0.5 bitcast_select_fusion
  143.3 2.4 bitcast_subtract_fusion
  145.7 3.9 fusion
  149.6 99.8 %collective-permute-done.1 = f32[512,2560]{1,0:T(8,128)} collective-permute-done((f32[512,2560]{1,0:T(8,128)}, f32[512,2560]{1,0:T(8,128)}, u32[]{:S(2)}, u32[]{:S(2)}) %collective-permute-start.1) | collective-permute-done | bytes 5242912 | tf_op jit(solution)/shard_map/ppermute | solution.py:59
  249.4 7.3 %add.89 = f32[512,2560]{1,0:T(8,128)} add(f32[512,2560]{1,0:T(8,128)} %add.88, f32[512,2560]{1,0:T(8,128)} %collective-permute-done.1) | non-fusion elementwise | flops 1310720 | bytes 15728640 | tf_op jit(solution)/shard_map/add | solution.py:59
  256.7 5.9 %copy.79 = f32[512,2560]{0,1:T(8,128)} copy(f32[512,2560]{1,0:T(8,128)} %add.89) | data formatting | bytes 10485760 | tf_op jit(solution)/shard_map/add | solution.py:59
  262.6 5.9 %copy.80 = f32[512,20,128]{2,0,1:T(8,128)} copy(f32[512,20,128]{0,2,1:T(8,128)} %bitcast.48) | data formatting | bytes 10485760 | tf_op jit(solution)/shard_map/reshape | solution.py:25
  268.6 5.7 gather_fusion.1
  274.2 5.9 %copy.81 = f32[512,20,128]{0,2,1:T(8,128)} copy(f32[512,20,128]{2,0,1:T(8,128)} %bitcast.47) | data formatting | bytes 10485760 | tf_op jit(solution)/shard_map/jit(_take)/gather | solution.py:26
  280.2 5.9 %copy.82 = f32[512,10,256]{2,0,1:T(8,128)} copy(f32[512,10,256]{0,2,1:T(8,128)} %bitcast.49) | data formatting | bytes 10485760 | tf_op jit(solution)/shard_map/jit(_take)/gather | solution.py:26
  286.1 2.9 broadcast_select_fusion
  289.0 2.3 copy-done.2
  291.3 2.8 fusion.11
  294.1 0.0 all-reduce.2.cloned.1.call-update
  294.1 1.5 copy.90
  295.6 2.9 fusion.33
  298.5 4.8 add_add_fusion
  303.3 3.2 gather_fusion
  306.4 3.4 gather_fusion.2
  309.8 4.7 fusion.7
  314.5 2.2 copy.97
  316.7 243.3 %all-reduce.2.cloned.1.call-done = f32[10,256,256]{2,1,0:T(8,128)} async-done(((f32[10,256,256]{2,1,0:T(8,128)}), f32[10,256,256]{2,1,0:T(8,128)}) %all-reduce.2.cloned.1.call-update) | async-done | bytes 2621456 | tf_op jit(solution)/shard_map/psum | solution.py:77
  560.1 4.9 fusion.2
  564.9 1.0 fusion.17
  566.0 1.0 fusion.19
  567.0 1.1 convolution_add_fusion.2
  568.1 0.9 convolution_add_fusion.1
  569.0 1.8 convolution_add_fusion
  570.8 2.3 copy.96
  573.1 1.5 fusion.14
  574.6 1.1 copy.98
  (23 shorter events, 0.2 us)
Async XLA Ops:
  7.2 129.7 %copy-start = (bf16[512,2560]{1,0:T(8,128)(2,1)S(1)}, bf16[512,2560]{1,0:T(8,128)(2,1)}, u32[]{:S(2)}) copy-start(bf16[512,2560]{1,0:T(8,128)(2,1)} %param.6) | copy-start | bytes 7864324
  7.2 552.9 %all-reduce.2.cloned.1.call-start = ((), (), s32[]{:S(2)}) async-start(), calls=%async_computation | async-start | bytes 5242880 | tf_op jit(solution)/shard_map/psum | solution.py:77
  15.5 114.9 %collective-permute-start = (f32[512,2560]{1,0:T(8,128)S(1)}, f32[512,2560]{1,0:T(8,128)S(1)}, u32[]{:S(2)}, u32[]{:S(2)}) collective-permute-start(f32[512,2560]{1,0:T(8,128)S(1)} %fusion.34), channel_id=1, source_target_pairs={{0,1},{1,0},{2,3},{3,2},{4,5},{5,4},{6,7},{7,6},{8,9},{9,8},{10,11... | collective-permute-start | bytes 15728648 | tf_op jit(solution)/shard_map/ppermute | solution.py:59
  133.7 3.9 copy-start.6
  133.7 115.7 %collective-permute-start.1 = (f32[512,2560]{1,0:T(8,128)}, f32[512,2560]{1,0:T(8,128)}, u32[]{:S(2)}, u32[]{:S(2)}) collective-permute-start(f32[512,2560]{1,0:T(8,128)} %add.88), channel_id=1, source_target_pairs={{0,2},{1,3},{2,0},{3,1},{4,6},{5,7},{6,4},{7,5},{8,10},{9,11},{10,... | collective-permute-start | bytes 15728648 | tf_op jit(solution)/shard_map/ppermute | solution.py:59
  136.9 2.0 copy-start.5
  140.7 2.1 copy-start.4
  289.0 2.3 copy-start.2
  316.7 248.2 %copy-start.3 = (f32[3,256,256]{2,0,1:T(4,128)S(1)}, f32[3,256,256]{2,0,1:T(4,128)}, u32[]{:S(2)}) copy-start(f32[3,256,256]{2,0,1:T(4,128)} %fusion) | copy-start | bytes 2359300
  569.0 6.7 %copy-start.1 = (bf16[512,2560]{1,0:T(8,128)(2,1)S(1)}, bf16[512,2560]{1,0:T(8,128)(2,1)}, u32[]{:S(2)}) copy-start(bf16[512,2560]{1,0:T(8,128)(2,1)} %param.6) | copy-start | bytes 7864324
Sparse Core Ops, SparseCore 0:
  294.2 265.8 all-reduce.1
